TPU v7x, 512 devices: a whole 4x4x16 slice. The times are simulated.
512 devices in a mesh: dp: 32 (over z, y_lo), expert: 16 (over x, y_hi, core).
Axes of the slice: x: 4, y: 4 (y_hi: 2, y_lo: 2; y = y_hi * 2 + y_lo), z: 16, core: 2. Of those that a mesh axis runs over, the one named last changes fastest.
Arguments:
- out_grad: bfloat16 [2048, 6144], P('expert', 'dp'), may hold values from -6 to 6
- hidden: bfloat16 [16, 1024, 5376], P('expert', None, 'dp'), may hold values from -0.59765625 to 0.59765625
- down_weight: bfloat16 [16, 5376, 6144], P('expert', 'dp'), may hold values from -0.078125 to 0.078125
- experts: int32 [2048, 4], replicated, may hold values from 0 to 15, all different within a row; in each aligned block of 128 rows (0 to 127, 128 to 255, ...) at most 64 rows name the same one
- route_weight: float32 [2048, 4], replicated, may hold values from 0.05 to 1
Outputs:
- hidden_grad: bfloat16 [16, 1024, 5376], P('expert', None, 'dp')
- weight_grad: bfloat16 [16, 5376, 6144], P('expert', 'dp')
- route_grad: float32 [2048, 4], P('expert')
Inputs may be any that keep to these rules, and one draw needn't show every extreme that they name: The 4 experts of a token differ; among the tokens of one aligned block of 128 tokens no expert is named by more than 64 of them.
All inputs are finite; a program needn't handle non-finite values.
Results may differ from a plain program's by a relative error of at most 0.0049.
Values may be sent and summed in bfloat16 or wider, within the bound.
A program may use at most 64 MiB of HBM per device.

v0:
```python
import jax
import jax.numpy as jnp
from jax import lax
from jax.sharding import PartitionSpec as P


def slot_table(experts, route_weight, expert_id, blocks, tok_dev, most):
    hit = experts == expert_id
    tok_hit = jnp.any(hit, axis=1).astype(jnp.int32)
    tok_weight = jnp.sum(jnp.where(hit, route_weight, 0.0), axis=1)
    block_hit = tok_hit.reshape(blocks, tok_dev)
    rank = jnp.cumsum(block_hit, axis=1) - 1
    marks = (block_hit[:, None, :] == 1) & (
        rank[:, None, :] == jnp.arange(most, dtype=jnp.int32)[None, :, None]
    )
    local = jnp.sum(
        jnp.where(marks, jnp.arange(tok_dev, dtype=jnp.int32)[None, None, :], 0), axis=2
    )
    live = jnp.any(marks, axis=2)
    slot_weight = jnp.sum(jnp.where(marks, tok_weight.reshape(blocks, 1, tok_dev), 0.0), axis=2)
    return (local, live, slot_weight, rank, hit)


def body(out_grad, hidden, down_weight, experts, route_weight):
    groups = lax.axis_size("expert")
    mine = lax.axis_index("expert")
    tok_dev = out_grad.shape[0]
    slots = hidden.shape[1]
    most = slots // groups
    local, live, slot_weight, rank, hit = slot_table(
        experts, route_weight, mine, groups, tok_dev, most
    )
    slot_weight = slot_weight.reshape(slots)
    live_flat = live.reshape(slots)
    matrix = down_weight[0]
    saved = hidden[0]
    whole = lax.all_gather(out_grad, "expert", axis=0, tiled=True)
    index = (jnp.arange(groups, dtype=jnp.int32)[:, None] * tok_dev + local).reshape(slots)
    part_rows = jnp.where(live_flat[:, None], whole[index], jnp.zeros((), whole.dtype))
    piece = lax.all_gather(part_rows, "dp", axis=1, tiled=True)
    raw_sum = lax.dot_general(
        piece, matrix, (((1,), (1,)), ((), ())), preferred_element_type=jnp.float32
    )
    scaled = (slot_weight[:, None] * piece.astype(jnp.float32)).astype(jnp.bfloat16)
    block_grad = lax.dot_general(
        saved, scaled, (((0,), (0,)), ((), ())), preferred_element_type=jnp.float32
    )
    hidden_grad = (slot_weight[:, None] * raw_sum).astype(jnp.bfloat16)
    weight_grad = block_grad.astype(jnp.bfloat16)
    partial_grad = jnp.sum(saved.astype(jnp.float32) * raw_sum, axis=1)
    slot_grad = lax.psum(partial_grad, "dp")
    tokens = experts.shape[0]
    block_ids = jnp.arange(tokens, dtype=jnp.int32) // tok_dev
    slot_index = block_ids * most + jnp.maximum(rank.reshape(tokens), 0)
    dense = jnp.where(hit, slot_grad[slot_index][:, None], 0.0)
    route_grad = lax.psum_scatter(dense, "expert", scatter_dimension=0, tiled=True)
    return (hidden_grad[None], weight_grad[None], route_grad)


def solution(mesh):
    placed = (P("expert", "dp"), P("expert", None, "dp"), P("expert", "dp", None), P(), P())
    return jax.shard_map(
        body,
        mesh=mesh,
        in_specs=placed,
        out_specs=(P("expert", None, "dp"), P("expert", "dp", None), P("expert", None)),
        check_vma=False,
    )
```

profile of v0, /device:TPU:1, one launch (start us, length us, event | category | flops | bytes accessed | tf_op | source)
XLA Modules:
  0.0 503.9 jit_solution(6056105228295138140)
XLA Ops:
  7.2 0.0 copy-start
  7.2 0.0 all-gather.2.cloned.1.call-start
  7.2 0.9 select_reduce_fusion.2
  8.2 0.3 reduce_window_sum.11
  8.5 0.3 select_reduce_fusion
  8.9 0.4 fusion.7
  9.2 0.1 broadcast_add_fusion
  9.3 0.1 add.83
  9.4 0.9 copy.12
  10.3 29.9 %all_gather.6 = bf16[2048,192]{1,0:T(8,128)(2,1)S(1)} all-gather(bf16[128,192]{1,0:T(8,128)(2,1)S(1)} %copy.12), channel_id=1, replica_groups=mesh['dp'=32,'expert'=16] {'expert'}, dimensions={0}, use_global_device_ids=true | all-gather | bytes 835584 | tf_op jit(solution)/shard_map/all_gather | solution.py:37
  40.2 0.1 broadcast_in_dim.71
  40.3 5.0 gather_fusion
  45.3 1.2 broadcast_select_fusion
  46.5 0.9 copy.13
  47.5 0.0 all-gather.2.cloned.1.call-update
  47.5 0.0 reduce-scatter.4.cloned.1.call-start
  47.6 0.2 select_reduce_fusion.1
  47.8 0.1 mul.42
  47.9 0.0 copy-start.1
  47.9 278.0 %all-gather.2.cloned.1.call-done = bf16[1024,6144]{0,1:T(8,128)(2,1)} async-done(((bf16[1024,192]{0,1:T(8,128)(2,1)}), bf16[1024,6144]{0,1:T(8,128)(2,1)}) %all-gather.2.cloned.1.call-update) | async-done | bytes 12582928 | tf_op jit(solution)/shard_map/all_gather | solution.py:40
  325.9 0.0 copy-done
  325.9 7.6 %multiply_reduce_fusion = (f32[1024]{0:T(1024)S(1)}, bf16[1,1024,168]{1,2,0:T(8,128)(2,1)}) fusion(bf16[1,1024,168]{1,2,0:T(8,128)(2,1)} %param.6, f32[1024]{0:T(1024)S(1)} %mul.42, bf16[1024,6144]{0,1:T(8,128)(2,1)} %all-gather.2.cloned.1.call-done, bf16[1,168,6144]{2,1,0:T(8,128)(2,1)S(1)} %copy-done), kind=kOutput, calls=%fused_computation.9 | convolution fusion | flops 2114788352 | bytes 15343616 | tf_op jit(solution)/shard_map/dot_general | solution.py:41
  333.5 50.4 %psum.7 = f32[1024]{0:T(1024)S(1)} all-reduce(f32[1024]{0:T(1024)S(1)} %get-tuple-element.5), channel_id=1, replica_groups=mesh['dp'=32,'expert'=16] {'dp'}, use_global_device_ids=true, to_apply=%region_7.8 | all-reduce | flops 1024 | bytes 8192 | tf_op jit(solution)/shard_map/psum | solution.py:51
  383.9 8.6 %gather_fusion.1 = f32[2048]{0:T(1024)S(1)} fusion(f32[1024]{0:T(1024)S(1)} %psum.7, s32[2048]{0:T(1024)S(1)} %broadcast_clamp_fusion), kind=kCustom, calls=%fused_computation.1 | custom fusion | bytes 24576 | tf_op jit(solution)/shard_map/gather | solution.py:55
  392.5 1.4 copy.14
  393.9 0.0 reduce-scatter.4.cloned.1.call-update
  394.0 0.0 copy-done.1
  394.0 10.2 %fusion.3 = bf16[1,168,6144]{2,1,0:T(8,128)(2,1)} fusion(bf16[1024,6144]{0,1:T(8,128)(2,1)} %all-gather.2.cloned.1.call-done, f32[1024]{0:T(1024)S(1)} %mul.42, bf16[1,1024,168]{1,2,0:T(8,128)(2,1)S(1)} %copy-done.1), kind=kOutput, calls=%fused_computation.6 | convolution fusion | flops 2133835776 | bytes 14995456 | tf_op jit(solution)/shard_map/dot_general | solution.py:45
  404.2 91.3 %reduce-scatter.4.cloned.1.call-done = f32[128,4]{1,0:T(8,128)} async-done(((f32[2048,4]{1,0:T(8,128)}), f32[128,4]{1,0:T(8,128)}) %reduce-scatter.4.cloned.1.call-update) | async-done | bytes 2064
  495.5 1.5 copy.15
  (10 shorter events, 0.1 us)
Async XLA Ops:
  7.2 318.7 %copy-start = (bf16[1,168,6144]{2,1,0:T(8,128)(2,1)S(1)}, bf16[1,168,6144]{2,1,0:T(8,128)(2,1)}, u32[]{:S(2)}) copy-start(bf16[1,168,6144]{2,1,0:T(8,128)(2,1)} %param.7) | copy-start | bytes 6193156
  7.2 318.7 %all-gather.2.cloned.1.call-start = ((), (), s32[]{:S(2)}) async-start(), calls=%async_computation.1 | async-start | bytes 12976128 | tf_op jit(solution)/shard_map/all_gather | solution.py:40
  47.5 448.0 %reduce-scatter.4.cloned.1.call-start = ((), (), s32[]{:S(2)}) async-start(), calls=%async_computation.2 | async-start | bytes 1114112
  47.9 346.1 %copy-start.1 = (bf16[1,1024,168]{1,2,0:T(8,128)(2,1)S(1)}, bf16[1,1024,168]{1,2,0:T(8,128)(2,1)}, u32[]{:S(2)}) copy-start(bf16[1,1024,168]{1,2,0:T(8,128)(2,1)} %param.6) | copy-start | bytes 1032196
Sparse Core Ops, SparseCore 0:
  47.6 278.2 all-gather.1
  394.1 101.4 reduce-scatter.3
where the time goes:
time: 505 us; the launch traced here: 504 us
  waiting for transfers between devices  369 us (73%)
  blocking collectives  80.3 us (16%)
  local copies, waits for them, and re-layouts  18.6 us (4%)
  matrix products  17.9 us (4%)
  between operations  14.2 us (3%)
    all_gather x1, waiting for transfers between devices, body(): piece = lax.all_gather(part_rows, 'dp', axis=1, tiled=True)  278 us
    unnamed x3, waiting for transfers between devices  91.4 us
    psum x1, blocking collectives, body(): slot_grad = lax.psum(partial_grad, 'dp')  50.4 us
    all_gather x1, blocking collectives, body(): whole = lax.all_gather(out_grad, 'expert', axis=0, tiled=True)  29.9 us
    dot_general x1, matrix products, body(): lax.dot_general(saved, scaled, (((0,), (0,)), ((), ())), preferred_elemen...  10.2 us
  transfers between devices with their start and end apart: 2, of which 2 were waited for; matrix products, arithmetic and copies ran while one was open for 2% of the time, Pallas kernels for 0%

commit v1 on v0

v1 whole, which is shorter than its diff:
```python
import functools

import jax
import jax.numpy as jnp
from jax import lax
from jax.experimental import pallas as pl
from jax.experimental.pallas import tpu as pltpu
from jax.sharding import PartitionSpec as P

MESH = pl.DeviceIdType.MESH
F32, BF16 = jnp.float32, jnp.bfloat16

X, Y, Z = 4, 4, 16
HALF = 64
FEAT = 384
BLOCKS = 16
TOK = 128
FFD = 168
MOST = 64
GROUPS = 9


def kernel(
    og_ref, hid_ref, w_ref, ex_ref, rw_ref,
    hg_ref, wg_ref, rt_ref,
    rows, raw, hwt, sel, code, wtok, half, sg, sgx, red,
    px_s, px_r, u_s, u_r, z_s, z_r, v_s, v_r, a_s, a_r, c_s, c_r, x_s, x_r, d_s, d_r,
):
    dp, ex = lax.axis_index("dp"), lax.axis_index("expert")
    z, ylo = dp // 2, dp % 2
    x, yhi, c = ex // 4, (ex // 2) % 2, ex % 2
    y = yhi * 2 + ylo
    u = y + c * (x - y)
    v = x + c * (y - x)

    def at(x, y, z, c):
        return {"dp": z * 2 + y % 2, "expert": (x * 2 + y // 2) * 2 + c}

    def along(du, dv):
        uu, vv = (u + du + 4) % 4, (v + dv + 4) % 4
        return at(vv + c * (uu - vv), uu + c * (vv - uu), z, c)

    def beside(dz):
        return at(x, y, (z + dz + Z) % Z, c)

    twin = at(x, y, z, 1 - c)
    pair = {"dp": dp + 1 - 2 * ylo, "expert": ex}

    barrier = pltpu.get_barrier_semaphore()
    greeted = [along(k, 0) for k in (1, 2, 3)] + [along(0, k) for k in (1, 2, 3)]
    greeted += [beside(1), beside(-1), twin]
    for device in greeted:
        pl.semaphore_signal(barrier, inc=1, device_id=device, device_id_type=MESH)
    pl.semaphore_wait(barrier, len(greeted))

    sent = []

    def copy(src, dst, send, recv, device):
        return pltpu.make_async_remote_copy(
            src_ref=src, dst_ref=dst, send_sem=send, recv_sem=recv, device_id=device, device_id_type=MESH
        )

    def push(src, dst, send, recv, device):
        op = copy(src, dst, send, recv, device)
        op.start()
        sent.append(op)

    def arrived(dst, send, recv):
        copy(dst, dst, send, recv, twin).wait_recv()

    push(og_ref.at[pl.ds((1 - ylo) * HALF, HALF)], half, px_s, px_r, pair)
    arrived(half, px_s, px_r)
    mine = og_ref[pl.ds(ylo * HALF, HALF), :].astype(F32)
    theirs = half[...].astype(F32)
    first = jnp.where(ylo == 0, mine, theirs)
    second = jnp.where(ylo == 0, theirs, mine)
    rows[0, c, v, u] = jnp.concatenate([first, second], axis=1).astype(BF16)

    for k in (1, 2, 3):
        own = rows.at[0, c, v, u]
        push(own, own, u_s.at[k - 1], u_r.at[k - 1], along(k, 0))
    for k in (1, 2, 3):
        arrived(rows.at[0, c, v, (u - k + 4) % 4], u_s.at[k - 1], u_r.at[k - 1])

    def z_part(slot, part):
        return rows.at[slot, c, v, pl.ds(2 * part, 2)]

    def z_send(d):
        for part in (0, 1):
            for way in (0, 1):
                if d == 7 and way != part:
                    continue
                src = 0 if d == 0 else 2 * d - 1 + way
                dst = 15 if d == 7 else 2 * d + 1 + way
                push(z_part(src, part), z_part(dst, part), z_s.at[d, way, part], z_r.at[d, way, part], beside(1 - 2 * way))

    def z_wait(d):
        for part in (0, 1):
            for way in (0, 1):
                if d == 8 and way != part:
                    continue
                dst = 15 if d == 8 else 2 * d - 1 + way
                arrived(z_part(dst, part), z_s.at[d - 1, way, part], z_r.at[d - 1, way, part])

    def slots(d):
        return pl.ds(0, 1) if d == 0 else pl.ds(15, 1) if d == 8 else pl.ds(2 * d - 1, 2)

    def v_all(d, vv):
        return rows.at[slots(d), c, vv]

    def v_half(d, vv, way):
        if d in (0, 8):
            return rows.at[slots(d), c, vv, pl.ds(2 * way, 2)]
        return rows.at[pl.ds(2 * d - 1 + way, 1), c, vv]

    def v_send(d):
        for way in (0, 1):
            own = v_all(d, v)
            push(own, own, v_s.at[d, way], v_r.at[d, way], along(0, 1 - 2 * way))

    def v_pass(d):
        for way in (0, 1):
            step = 1 - 2 * way
            vv = (v - step + 4) % 4
            arrived(v_all(d, vv), v_s.at[d, way], v_r.at[d, way])
            part = v_half(d, vv, way)
            push(part, part, a_s.at[d, way], a_r.at[d, way], along(0, step))

    def c_send(d):
        vv = (v + 2) % 4
        for way in (0, 1):
            arrived(v_half(d, vv, way), a_s.at[d, way], a_r.at[d, way])
        own = rows.at[slots(d), c]
        push(own, own, c_s.at[d], c_r.at[d], twin)

    def c_wait(d):
        arrived(rows.at[slots(d), 1 - c], c_s.at[d], c_r.at[d])

    def prepare():
        hit = jnp.zeros((BLOCKS, TOK), jnp.bool_)
        weight = jnp.zeros((BLOCKS, TOK), F32)
        for k in range(4):
            mine = ex_ref[k] == ex
            hit = hit | mine
            weight = weight + jnp.where(mine, rw_ref[k], 0.0)
        upto = lax.broadcasted_iota(jnp.int32, (TOK, TOK), 0) <= lax.broadcasted_iota(jnp.int32, (TOK, TOK), 1)
        count = jnp.dot(
            jnp.where(hit, 1.0, 0.0).astype(BF16), jnp.where(upto, 1.0, 0.0).astype(BF16), preferred_element_type=F32
        )
        code[...] = jnp.where(hit, count - 1.0, -1.0)
        wtok[...] = weight
        slot = lax.broadcasted_iota(jnp.int32, (MOST, TOK), 0).astype(F32)
        lane = lax.broadcasted_iota(jnp.int32, (FFD, TOK), 1)

        def block(b):
            one = jnp.where(slot == code[pl.ds(b, 1), :], 1.0, 0.0)
            sel[b] = one.astype(BF16)
            w = jnp.sum(one * wtok[pl.ds(b, 1), :], axis=1, keepdims=True)
            hid = hid_ref[0, pl.ds(b * MOST, MOST), :]
            hidw = (hid.astype(F32) * w).astype(BF16)
            return lax.dot_general(hidw, one.astype(BF16), (((0,), (0,)), ((), ())), preferred_element_type=F32)

        def plane0(i, _):
            hwt[i] = block(i * 2).astype(BF16)
            return 0

        lax.fori_loop(0, 8, plane0, 0)

        def plane1(i, _):
            xh, yh = i // 2, i % 2
            b0 = xh * 8 + yh * 2 + 1
            left, right = block(b0), block(b0 + 4)
            low = jnp.where(lane < HALF, left, pltpu.roll(right, HALF, 1))
            high = jnp.where(lane < HALF, pltpu.roll(left, HALF, 1), right)
            hwt[8 + yh * 4 + xh] = low.astype(BF16)
            hwt[8 + yh * 4 + 2 + xh] = high.astype(BF16)
            return 0

        lax.fori_loop(0, 4, plane1, 0)
        raw[...] = jnp.zeros_like(raw)

    def places(d):
        if d == 0:
            return ((0, z),)
        if d == 8:
            return ((15, (z + 8) % Z),)
        return ((2 * d - 1, (z - d + Z) % Z), (2 * d, (z + d) % Z))

    def columns(zi):
        return pl.ds(pl.multiple_of(zi * FEAT, 128), FEAT)

    def add_raw(d):
        here = places(d)
        w = jnp.concatenate([w_ref[0, :, columns(zi)] for _, zi in here], axis=1)

        def tile(i, _):
            t = jnp.concatenate([rows[s, i // 4, i % 4].reshape(4 * HALF, FEAT) for s, _ in here], axis=1)
            raw[i] += lax.dot_general(t, w, (((1,), (1,)), ((), ())), preferred_element_type=F32)
            return 0

        lax.fori_loop(0, 8, tile, 0)

    def put_grad(d):
        for s, zi in places(d):
            left = jnp.concatenate([hwt[i] for i in range(16)], axis=1)
            t = rows[s].reshape(2 * X * Y * HALF, FEAT)
            wg_ref[0, :, columns(zi)] = jnp.dot(left, t, preferred_element_type=F32).astype(BF16)

    z_send(0)
    v_send(0)
    prepare()
    for d in range(1, GROUPS + 3):
        if d <= 8:
            z_wait(d)
            if d < 8:
                z_send(d)
            v_send(d)
        if 0 <= d - 1 <= 8:
            v_pass(d - 1)
        if 0 <= d - 2 <= 8:
            c_send(d - 2)
        if 0 <= d - 3 <= 8:
            c_wait(d - 3)
            add_raw(d - 3)
            if d - 3 < 8:
                put_grad(d - 3)

    def block_out(b, row0, row1):
        part = jnp.concatenate([row0, row1], axis=0)
        high = part.astype(BF16)
        low = (part - high.astype(F32)).astype(BF16)
        one = sel[b]
        mine = jnp.dot(one, high, preferred_element_type=F32) + jnp.dot(one, low, preferred_element_type=F32)
        onef = one.astype(F32)
        w = jnp.sum(onef * wtok[pl.ds(b, 1), :], axis=1, keepdims=True)
        at_b = pl.ds(b * MOST, MOST)
        hg_ref[0, at_b, :] = (w * mine).astype(BF16)
        slot_grad = jnp.sum(hid_ref[0, at_b, :].astype(F32) * mine, axis=1, keepdims=True)
        sg[b] = jnp.broadcast_to(jnp.sum(slot_grad * onef, axis=0, keepdims=True), (8, TOK))

    def out0(i, _):
        at_i = pl.multiple_of((i % 2) * TOK, TOK)
        block_out(i * 2, raw[i // 2, pl.ds(at_i, HALF), :], raw[i // 2, pl.ds(at_i + HALF, HALF), :])
        return 0

    def out1(i, _):
        xx, yh = i // 2, i % 2
        at_i = pl.multiple_of(xx * HALF, HALF)
        block_out(i * 2 + 1, raw[4 + 2 * yh, pl.ds(at_i, HALF), :], raw[5 + 2 * yh, pl.ds(at_i, HALF), :])
        return 0

    lax.fori_loop(0, 8, out0, 0)
    lax.fori_loop(0, 8, out1, 0)

    for k in range(1, BLOCKS):
        to = (ex + k) % BLOCKS
        push(sg.at[to], sgx.at[ex], x_s.at[k], x_r.at[k], {"dp": dp, "expert": to})
    put_grad(8)
    sgx[ex] = sg[ex]
    for k in range(1, BLOCKS):
        arrived(sgx.at[(ex - k + BLOCKS) % BLOCKS], x_s.at[k], x_r.at[k])
    share = []
    for k in range(4):
        named = ex_ref[k, pl.ds(ex, 1), :]
        total = jnp.zeros((1, TOK), F32)
        for e in range(BLOCKS):
            total = total + jnp.where(named == e, sgx[e, 0:1, :], 0.0)
        share.append(total)
    red[dp] = jnp.concatenate(share, axis=0)
    for k in range(1, 2 * Z):
        own = red.at[dp]
        push(own, own, d_s.at[k], d_r.at[k], {"dp": (dp + k) % (2 * Z), "expert": ex})
    for k in range(1, 2 * Z):
        arrived(red.at[(dp - k + 2 * Z) % (2 * Z)], d_s.at[k], d_r.at[k])
    total = red[0]
    for k in range(1, 2 * Z):
        total = total + red[k]
    rt_ref[...] = total
    for op in sent:
        op.wait_send()


def body(out_grad, hidden, down_weight, experts, route_weight):
    experts_t = experts.T.reshape(4, BLOCKS, TOK)
    weight_t = route_weight.T.reshape(4, BLOCKS, TOK)
    vmem = pl.BlockSpec(memory_space=pltpu.VMEM)
    dma = pltpu.SemaphoreType.DMA
    hidden_grad, weight_grad, route = pl.pallas_call(
        kernel,
        out_shape=(
            jax.ShapeDtypeStruct(hidden.shape, BF16),
            jax.ShapeDtypeStruct(down_weight.shape, BF16),
            jax.ShapeDtypeStruct((4, TOK), F32),
        ),
        in_specs=[vmem] * 5,
        out_specs=(vmem,) * 3,
        scratch_shapes=[
            pltpu.VMEM((Z, 2, 4, 4, HALF, FEAT), BF16),
            pltpu.VMEM((8, 4 * HALF, FFD), F32),
            pltpu.VMEM((16, FFD, TOK), BF16),
            pltpu.VMEM((BLOCKS, MOST, TOK), BF16),
            pltpu.VMEM((BLOCKS, TOK), F32),
            pltpu.VMEM((BLOCKS, TOK), F32),
            pltpu.VMEM((HALF, 192), BF16),
            pltpu.VMEM((BLOCKS, 8, TOK), F32),
            pltpu.VMEM((BLOCKS, 8, TOK), F32),
            pltpu.VMEM((2 * Z, 4, TOK), F32),
            dma, dma,
            dma((3,)), dma((3,)),
            dma((8, 2, 2)), dma((8, 2, 2)),
            dma((GROUPS, 2)), dma((GROUPS, 2)),
            dma((GROUPS, 2)), dma((GROUPS, 2)),
            dma((GROUPS,)), dma((GROUPS,)),
            dma((BLOCKS,)), dma((BLOCKS,)),
            dma((2 * Z,)), dma((2 * Z,)),
        ],
        compiler_params=pltpu.CompilerParams(
            collective_id=0, has_side_effects=True, vmem_limit_bytes=56 << 20
        ),
        cost_estimate=pl.CostEstimate(flops=8 * 10**9, bytes_accessed=30 * 10**6, transcendentals=0),
        name="broadcast_grads",
    )(out_grad, hidden, down_weight, experts_t, weight_t)
    return hidden_grad, weight_grad, route.T


def solution(mesh):
    placed = (P("expert", "dp"), P("expert", None, "dp"), P("expert", "dp", None), P(), P())
    return jax.shard_map(
        body,
        mesh=mesh,
        in_specs=placed,
        out_specs=(P("expert", None, "dp"), P("expert", "dp", None), P("expert", None)),
        check_vma=False,
    )
```

time: 505 us -> 124 us (0.25)
  waiting for transfers between devices: 369 us -> 0 us
  Pallas kernels: 0 us -> 111 us
  blocking collectives: 80.3 us -> 0 us
  matrix products: 17.9 us -> 0 us
  between operations: 14.2 us -> 0.64 us
  local copies, waits for them, and re-layouts: 18.6 us -> 11.9 us
    all_gather x1 -> x0, waiting for transfers between devices: 278 us -> none  [body(): piece = lax.all_gather(part_rows, 'dp', axis=1, tiled=True)]
    pallas_call x0 -> x1, Pallas kernels: none -> 111 us  [body(): pl.pallas_call(kernel, out_shape=(jax.ShapeDtypeStruct(hidden.shape, BF16...]
    unnamed x3 -> x0, waiting for transfers between devices: 91.4 us -> none
    psum x1 -> x0, blocking collectives: 50.4 us -> none  [body(): slot_grad = lax.psum(partial_grad, 'dp')]
    all_gather x1 -> x0, blocking collectives: 29.9 us -> none  [body(): whole = lax.all_gather(out_grad, 'expert', axis=0, tiled=True)]
    dot_general x2 -> x0, matrix products: 17.9 us -> none  [the longest x1 10.2 us: body(): lax.dot_general(saved, scaled, (((0,), (0,)), ((), ())), preferred_elemen...]
    gather x2 -> x0, local copies, waits for them, and re-layouts: 13.6 us -> none  [the longest x1 8.58 us: body(): dense = jnp.where(hit, slot_grad[slot_index][:, None], 0.0)]
    unnamed x7 -> x9, local copies, waits for them, and re-layouts: 3.83 us -> 11.9 us
  transfers between devices with their start and end apart: 2 -> 0, of which waited for: 2 -> 0; matrix products, arithmetic and copies ran while one was open for 2% -> 0% of each run, Pallas kernels for 0% -> 0%
where the time goes in v1:
time: 124 us
  Pallas kernels  111 us (90%)
  local copies, waits for them, and re-layouts  11.9 us (10%)
    pallas_call x1, Pallas kernels, body(): pl.pallas_call(kernel, out_shape=(jax.ShapeDtypeStruct(hidden.shape, BF16...  111 us
    unnamed x9, local copies, waits for them, and re-layouts  11.9 us

profile of v1, /device:TPU:1, one launch (start us, length us, event | category | flops | bytes accessed | tf_op | source)
XLA Modules:
  0.0 123.5 jit_solution(13004464066689743212)
XLA Ops:
  0.6 1.4 %copy.16 = s32[1,4,16,128]{3,2,1,0:T(8,128)} copy(s32[1,4,16,128]{3,1,2,0:T(4,128)} %bitcast.11) | data formatting | bytes 65536
  2.0 1.4 %copy.15 = f32[1,4,16,128]{3,2,1,0:T(8,128)} copy(f32[1,4,16,128]{3,1,2,0:T(4,128)} %bitcast.12) | data formatting | bytes 65536
  3.4 1.5 %copy.8.og_ref = bf16[128,192]{1,0:T(8,128)(2,1)} copy(bf16[128,192]{0,1:T(8,128)(2,1)} %param.5) | data formatting | bytes 98304 | tf_op args[0]
  4.9 2.0 %copy.9.hid_ref = bf16[1,1024,168]{2,1,0:T(8,128)(2,1)} copy(bf16[1,1024,168]{1,2,0:T(8,128)(2,1)} %param.6) | data formatting | bytes 688128 | tf_op args[1]
  6.9 111.0 %broadcast_grads.1 = (bf16[1,1024,168]{2,1,0:T(8,128)(2,1)}, bf16[1,168,6144]{2,1,0:T(8,128)(2,1)}, f32[4,128]{1,0:T(4,128)}) custom-call(bf16[128,192]{1,0:T(8,128)(2,1)} %copy.8.og_ref, bf16[1,1024,168]{2,1,0:T(8,128)(2,1)} %copy.9.hid_ref, bf16[1,168,6144]{2,1,0:T(8,128)(2,1)} %w_ref.1, s32[4,16,128]{2,1,0:T(8,128)} %bitcast.13, f32[4,16,128]{2,1,0:T(8,128)} %bitcast.14), custom_call_target="tpu_custom_call" | custom-call | flops 8000000000 | bytes 30000000 | tf_op jit(solution)/shard_map/broadcast_grads/pallas_call | solution.py:288
  117.9 2.0 %copy.10 = bf16[1,1024,168]{1,2,0:T(8,128)(2,1)} copy(bf16[1,1024,168]{2,1,0:T(8,128)(2,1)} %get-tuple-element.9) | data formatting | bytes 688128
  119.8 0.0 copy-start
  119.8 3.1 %copy.19 = bf16[1,168,6144]{2,1,0:T(8,128)(2,1)} copy(bf16[1,168,6144]{2,1,0:T(8,128)(2,1)} %get-tuple-element.16) | data formatting | bytes 4128768
  122.9 0.0 copy-done
  122.9 0.6 copy.20
Async XLA Ops:
  119.8 3.1 %copy-start = (f32[4,128]{1,0:T(4,128)S(1)}, f32[4,128]{1,0:T(4,128)}, u32[]{:S(2)}) copy-start(f32[4,128]{1,0:T(4,128)} %get-tuple-element.8) | copy-start | bytes 6148

commit v2 on v1

v2 whole, which is shorter than its diff:
```python
import jax
import jax.numpy as jnp
from jax import lax
from jax.experimental import pallas as pl
from jax.experimental.pallas import tpu as pltpu
from jax.sharding import PartitionSpec as P

MESH = pl.DeviceIdType.MESH
F32, BF16 = jnp.float32, jnp.bfloat16

Z = 16
PIECE = 192
FEAT = 384
BLOCKS = 16
TOK = 128
TOKENS = BLOCKS * TOK
FFD = 168
MOST = 64
GROUPS = 9
NT = (((1,), (1,)), ((), ()))
ORDER = (0, 1, 3, 2)
EARLY = (0, 1, 2)
EARLY_SLOTS = (0, 1, 2, 3, 4)
SKIP = 4
LATE = (4, 7, 8)

PLAN = (
    "U1", "U3", "Z10", "U2", "Z11", "Z13", "P0", "Z12", "Z20", "Z21", "Z23", "L0", "Z22", "P1", "Z30", "Z31", "R0",
    "Z33", "G0", "Z32", "P2", "Z40", "L1", "Z41", "Z43", "Z42", "R1", "Z50", "Z51", "P3", "Z53", "G1", "Z52", "L2",
    "E0", "Z60", "Z61", "L3", "R2", "Z63", "Z62", "R3", "P5", "Z70", "E1", "F0", "G2", "Z71", "E2", "G3", "Z73", "Z72",
    "Z80", "P6", "E3", "F1", "L5", "Z81", "E4", "Z83", "F2", "Z82", "R5", "P7", "E5", "F3", "G5", "L6", "F4", "P8",
    "R6", "F5", "L7", "G6", "L8", "R4", "R7", "R8",
)


def kernel(
    og_ref, hid_hbm, w_hbm, ex_hbm, rw_hbm,
    hg_ref, wg_ref, rt_ref,
    hid_ref, w_ref, ex_ref, rw_ref,
    rows, raw, ht, hw, sel, wtok, sg, sgx, red,
    load, u_s, u_r, z_s, z_r, p_s, p_r, e_s, e_r, v_s, v_r, a_s, a_r, c_s, c_r, x_s, x_r, d_s, d_r,
):
    dp, ex = lax.axis_index("dp"), lax.axis_index("expert")
    z, ylo = dp // 2, dp % 2
    x, yhi, c = ex // 4, (ex // 2) % 2, ex % 2
    y = yhi * 2 + ylo
    u = y + c * (x - y)
    v = x + c * (y - x)

    def at(x, y, z, c):
        return {"dp": z * 2 + y % 2, "expert": (x * 2 + y // 2) * 2 + c}

    def along(du, dv):
        uu, vv = (u + du + 4) % 4, (v + dv + 4) % 4
        return at(vv + c * (uu - vv), uu + c * (vv - uu), z, c)

    def beside(dz):
        return at(x, y, (z + dz + Z) % Z, c)

    twin = at(x, y, z, 1 - c)

    loads = [
        pltpu.make_async_copy(src, dst, load.at[i])
        for i, (src, dst) in enumerate(
            ((ex_hbm, ex_ref), (rw_hbm, rw_ref), (hid_hbm, hid_ref), (w_hbm, w_ref))
        )
    ]
    for op in loads:
        op.start()

    barrier = pltpu.get_barrier_semaphore()
    greeted = [along(k, 0) for k in (1, 2, 3)] + [along(0, k) for k in (1, 3)]
    greeted += [beside(1), beside(-1), twin]
    for device in greeted:
        pl.semaphore_signal(barrier, inc=1, device_id=device, device_id_type=MESH)
    pl.semaphore_wait(barrier, len(greeted))

    sent = []

    def copy(src, dst, send, recv, device):
        return pltpu.make_async_remote_copy(
            src_ref=src, dst_ref=dst, send_sem=send, recv_sem=recv, device_id=device, device_id_type=MESH
        )

    def push(src, dst, send, recv, device):
        op = copy(src, dst, send, recv, device)
        op.start()
        sent.append(op)

    def arrived(dst, send, recv):
        copy(dst, dst, send, recv, twin).wait_recv()


    def piece(slot, vv, k):
        return rows.at[slot, c, vv, (u - k + 4) % 4]

    def z_send(d, k):
        for way in (0, 1):
            if d == 7 and way != k // 2:
                continue
            src = 0 if d == 0 else 2 * d - 1 + way
            dst = 15 if d == 7 else 2 * d + 1 + way
            own = og_ref if d == 0 and k == 0 else piece(src, v, k)
            push(own, piece(dst, v, k), z_s.at[d, way, k], z_r.at[d, way, k], beside(1 - 2 * way))

    def z_wait(d, k):
        for way in (0, 1):
            if d == 8 and way != k // 2:
                continue
            dst = 15 if d == 8 else 2 * d - 1 + way
            arrived(piece(dst, v, k), z_s.at[d - 1, way, k], z_r.at[d - 1, way, k])

    def slot_list(d):
        return (0,) if d == 0 else (15,) if d == 8 else (2 * d - 1, 2 * d)

    def slots(d):
        return pl.ds(0, 1) if d == 0 else pl.ds(15, 1) if d == 8 else pl.ds(2 * d - 1, 2)

    def v_all(d, vv):
        return rows.at[slots(d), c, vv]

    def v_half(d, vv, way):
        if d in (0, 8):
            return rows.at[slots(d), c, vv, pl.ds(2 * way, 2)]
        return rows.at[pl.ds(2 * d - 1 + way, 1), c, vv]

    def v_send(d):
        for way in (0, 1):
            own = v_all(d, v)
            push(own, own, v_s.at[d, way], v_r.at[d, way], along(0, 1 - 2 * way))

    def v_piece(slot, k):
        at_slot = EARLY_SLOTS.index(slot)
        for way in (0, 1):
            own = og_ref if slot == 0 and k == 0 else piece(slot, v, k)
            push(own, piece(slot, v, k), p_s.at[at_slot, k, way], p_r.at[at_slot, k, way], along(0, 1 - 2 * way))

    def v_pass(d):
        for way in (0, 1):
            step = 1 - 2 * way
            vv = (v - step + 4) % 4
            if d in EARLY:
                for slot in slot_list(d):
                    for k in ORDER:
                        at_slot = EARLY_SLOTS.index(slot)
                        arrived(piece(slot, vv, k), p_s.at[at_slot, k, way], p_r.at[at_slot, k, way])
            else:
                arrived(v_all(d, vv), v_s.at[d, way], v_r.at[d, way])
            half = v_half(d, vv, way)
            push(half, half, a_s.at[d, way], a_r.at[d, way], along(0, step))

    def v_last(d):
        for way in (0, 1):
            arrived(v_half(d, (v + 2) % 4, way), a_s.at[d, way], a_r.at[d, way])

    def e_part(slot, unit):
        return rows.at[slot, c, (v + (1, 3, 2)[unit // 2]) % 4, pl.ds(2 * (unit % 2), 2)]

    def e_send(unit):
        for way in (0, 1):
            src, dst = e_part(2 * SKIP - 3 + way, unit), e_part(2 * SKIP - 1 + way, unit)
            push(src, dst, e_s.at[way, unit], e_r.at[way, unit], beside(1 - 2 * way))

    def e_wait(unit):
        for way in (0, 1):
            arrived(e_part(2 * SKIP - 1 + way, unit), e_s.at[way, unit], e_r.at[way, unit])

    def c_send(d, k):
        own = rows.at[slots(d), c, (v + k) % 4]
        push(own, own, c_s.at[d, k], c_r.at[d, k], twin)

    def c_wait(d):
        for k in range(4):
            arrived(rows.at[slots(d), 1 - c, (u + k) % 4], c_s.at[d, k], c_r.at[d, k])

    def prepare():
        mine = ex_ref[...] == ex
        hit = jnp.max(jnp.where(mine, 1.0, 0.0), axis=0, keepdims=True)
        wtok[...] = jnp.sum(jnp.where(mine, rw_ref[...], 0.0), axis=0, keepdims=True)
        hits = jnp.concatenate([hit[:, b * TOK : (b + 1) * TOK] for b in range(BLOCKS)], axis=0)
        upto = lax.broadcasted_iota(jnp.int32, (TOK, TOK), 0) <= lax.broadcasted_iota(jnp.int32, (TOK, TOK), 1)
        count = jnp.dot(hits.astype(BF16), jnp.where(upto, 1.0, 0.0).astype(BF16), preferred_element_type=F32)
        code = jnp.where(hits > 0, count - 1.0, -1000.0)
        slot = lax.broadcasted_iota(jnp.int32, (2 * MOST, 2 * TOK), 0).astype(F32)
        for j in range(BLOCKS // 2):
            both = jnp.concatenate([code[2 * j : 2 * j + 1], code[2 * j + 1 : 2 * j + 2] + float(MOST)], axis=1)
            one = jnp.where(slot == both, 1.0, 0.0).astype(BF16)
            sel[j] = one
            tokens = pl.ds(j * 2 * TOK, 2 * TOK)
            part = jnp.dot(hid_ref[0, :, pl.ds(j * TOK, TOK)], one, preferred_element_type=F32)
            ht[:, tokens] = part.astype(BF16)
            hw[:, tokens] = (part * wtok[:, tokens]).astype(BF16)

    def places(d):
        if d == 0:
            return ((0, z),)
        if d == 8:
            return ((15, (z + 8) % Z),)
        return ((2 * d - 1, (z - d + Z) % Z), (2 * d, (z + d) % Z))

    def columns(zi):
        return pl.ds(pl.multiple_of(zi * FEAT, 128), FEAT)

    def slab(s, xx):
        cols = []
        for b in range(4):
            yh = b // 2
            if b % 2 == 0:
                cols.append(rows[s, 0, xx, 2 * yh : 2 * yh + 2].reshape(FEAT, TOK))
            else:
                cols.append(jnp.concatenate([rows[s, 1, 2 * yh, xx], rows[s, 1, 2 * yh + 1, xx]], axis=0))
        return jnp.concatenate(cols, axis=1)

    def add_raw(d, first):
        here = places(d)
        w = jnp.concatenate([w_ref[0, :, columns(zi)] for _, zi in here], axis=1)

        def tile(xx, _):
            t = jnp.concatenate([slab(s, xx) for s, _ in here], axis=0)
            tokens = pl.ds(pl.multiple_of(xx * 4 * TOK, 4 * TOK), 4 * TOK)
            more = jnp.dot(w, t, preferred_element_type=F32)
            raw[:, tokens] = more if first else raw[:, tokens] + more
            return 0

        lax.fori_loop(0, 4, tile, 0)

    def put_grad(d):
        for s, zi in places(d):
            t = jnp.concatenate([slab(s, xx) for xx in range(4)], axis=1)
            wg_ref[0, :, columns(zi)] = lax.dot_general(hw[...], t, NT, preferred_element_type=F32).astype(BF16)

    for k in (1, 3, 2):
        push(og_ref, piece(0, v, 0), u_s.at[k - 1], u_r.at[k - 1], along(k, 0))
    z_send(0, 0)
    v_piece(0, 0)
    rows[0, c, v, u] = og_ref[...]
    for op in loads[:3]:
        op.wait()
    prepare()
    loads[3].wait()

    def on_u(k):
        arrived(piece(0, v, k), u_s.at[k - 1], u_r.at[k - 1])
        z_send(0, k)
        v_piece(0, k)
        if k == ORDER[3]:
            c_send(0, 0)

    def on_z(d, k):
        z_wait(d, k)
        if d < 8:
            z_send(d, k)
        if d in EARLY:
            for slot in slot_list(d):
                v_piece(slot, k)
        if k == ORDER[3]:
            if d not in EARLY and d != SKIP:
                v_send(d)
            c_send(d, 0)

    def on_v(d):
        v_pass(d)
        c_send(d, 1)
        c_send(d, 3)

    def on_far(d):
        v_last(d)
        c_send(d, 2)

    def on_e(unit):
        e_wait(unit)
        if unit % 2 == 1:
            c_send(SKIP, (1, 3, 2)[unit // 2])

    summed = []
    for step in PLAN:
        kind, d = step[0], int(step[1])
        if kind == "U":
            on_u(d)
        elif kind == "Z":
            on_z(d, int(step[2]))
        elif kind == "P":
            on_v(d)
        elif kind == "L":
            on_far(d)
        elif kind == "E":
            e_send(d)
        elif kind == "F":
            on_e(d)
        elif kind == "R":
            c_wait(d)
            add_raw(d, not summed)
            summed.append(d)
        else:
            put_grad(d)

    share = jnp.sum(ht[...].astype(F32) * raw[...], axis=0, keepdims=True)
    for b in range(BLOCKS):
        sg[b] = jnp.broadcast_to(share[:, b * TOK : (b + 1) * TOK], (8, TOK))
    for k in range(1, BLOCKS):
        to = (ex + k) % BLOCKS
        push(sg.at[to], sgx.at[ex], x_s.at[k], x_r.at[k], {"dp": dp, "expert": to})
    sgx[ex] = sg[ex]
    for d in LATE[::2]:
        put_grad(d)
    named = ex_ref[:, pl.ds(pl.multiple_of(ex * TOK, TOK), TOK)]
    total = jnp.zeros((4, TOK), F32)
    for k in range(1, BLOCKS):
        arrived(sgx.at[(ex - k + BLOCKS) % BLOCKS], x_s.at[k], x_r.at[k])
    for e in range(BLOCKS):
        total = total + jnp.where(named == e, sgx[e, 0:1, :], 0.0)
    red[dp] = total
    for k in range(1, 2 * Z):
        push(red.at[dp], red.at[dp], d_s.at[k], d_r.at[k], {"dp": (dp + k) % (2 * Z), "expert": ex})
    for d in LATE[1::2]:
        put_grad(d)
    for j in range(BLOCKS // 2):
        tokens = pl.ds(j * 2 * TOK, 2 * TOK)
        grad = (raw[:, tokens] * wtok[:, tokens]).astype(BF16)
        hg_ref[0, :, pl.ds(j * TOK, TOK)] = lax.dot_general(grad, sel[j], NT, preferred_element_type=F32).astype(BF16)
    for k in range(1, 2 * Z):
        arrived(red.at[(dp - k + 2 * Z) % (2 * Z)], d_s.at[k], d_r.at[k])
    total = red[0]
    for k in range(1, 2 * Z):
        total = total + red[k]
    rt_ref[...] = total
    for op in sent:
        op.wait_send()


def body(out_grad, hidden, down_weight, experts, route_weight):
    vmem = pl.BlockSpec(memory_space=pltpu.VMEM)
    dma = pltpu.SemaphoreType.DMA
    hidden_grad, weight_grad, route = pl.pallas_call(
        kernel,
        out_shape=(
            jax.ShapeDtypeStruct((1, FFD, BLOCKS * MOST), BF16),
            jax.ShapeDtypeStruct(down_weight.shape, BF16),
            jax.ShapeDtypeStruct((4, TOK), F32),
        ),
        in_specs=[vmem] + [pl.BlockSpec(memory_space=pltpu.HBM)] * 4,
        out_specs=(vmem,) * 3,
        scratch_shapes=[
            pltpu.VMEM((1, FFD, BLOCKS * MOST), BF16),
            pltpu.VMEM(down_weight.shape, BF16),
            pltpu.VMEM((4, TOKENS), jnp.int32),
            pltpu.VMEM((4, TOKENS), F32),
            pltpu.VMEM((Z, 2, 4, 4, PIECE, TOK), BF16),
            pltpu.VMEM((FFD, TOKENS), F32),
            pltpu.VMEM((FFD, TOKENS), BF16),
            pltpu.VMEM((FFD, TOKENS), BF16),
            pltpu.VMEM((BLOCKS // 2, 2 * MOST, 2 * TOK), BF16),
            pltpu.VMEM((1, TOKENS), F32),
            pltpu.VMEM((BLOCKS, 8, TOK), F32),
            pltpu.VMEM((BLOCKS, 8, TOK), F32),
            pltpu.VMEM((2 * Z, 4, TOK), F32),
            dma((4,)),
            dma((3,)), dma((3,)),
            dma((8, 2, 4)), dma((8, 2, 4)),
            dma((5, 4, 2)), dma((5, 4, 2)),
            dma((2, 6)), dma((2, 6)),
            dma((GROUPS, 2)), dma((GROUPS, 2)),
            dma((GROUPS, 2)), dma((GROUPS, 2)),
            dma((GROUPS, 4)), dma((GROUPS, 4)),
            dma((BLOCKS,)), dma((BLOCKS,)),
            dma((2 * Z,)), dma((2 * Z,)),
        ],
        compiler_params=pltpu.CompilerParams(
            collective_id=0, has_side_effects=True, vmem_limit_bytes=42 << 20
        ),
        cost_estimate=pl.CostEstimate(flops=8 * 10**9, bytes_accessed=30 * 10**6, transcendentals=0),
        name="broadcast_grads",
    )(out_grad.T, hidden.swapaxes(1, 2), down_weight, experts.T, route_weight.T)
    return hidden_grad.swapaxes(1, 2), weight_grad, route.T


def solution(mesh):
    placed = (P("expert", "dp"), P("expert", None, "dp"), P("expert", "dp", None), P(), P())
    return jax.shard_map(
        body,
        mesh=mesh,
        in_specs=placed,
        out_specs=(P("expert", None, "dp"), P("expert", "dp", None), P("expert", None)),
        check_vma=False,
    )
```

time: 124 us -> 97.5 us (0.79)
  Pallas kernels: 111 us -> 88.8 us
  local copies, waits for them, and re-layouts: 11.9 us -> 7.48 us
    pallas_call x1, Pallas kernels: 111 us -> 88.8 us  [body(): pl.pallas_call(kernel, out_shape=(jax.ShapeDtypeStruct((1, FFD, BLOCKS *...]
    unnamed x9 -> x13, local copies, waits for them, and re-layouts: 11.9 us -> 7.48 us
where the time goes in v2:
time: 97.5 us; the launch traced here: 96.9 us
  Pallas kernels  88.8 us (91%)
  local copies, waits for them, and re-layouts  7.48 us (8%)
    pallas_call x1, Pallas kernels, body(): pl.pallas_call(kernel, out_shape=(jax.ShapeDtypeStruct((1, FFD, BLOCKS *...  88.8 us
    unnamed x13, local copies, waits for them, and re-layouts  7.48 us

profile of v2, /device:TPU:1, one launch (start us, length us, event | category | flops | bytes accessed | tf_op | source)
XLA Modules:
  0.0 96.9 jit_solution(10230982519637630569)
XLA Ops:
  0.6 0.0 copy-start
  0.6 1.6 %copy-done = bf16[1,168,6144]{2,1,0:T(8,128)(2,1)S(1)} copy-done((bf16[1,168,6144]{2,1,0:T(8,128)(2,1)S(1)}, bf16[1,168,6144]{2,1,0:T(8,128)(2,1)}, u32[]{:S(2)}) %copy-start) | copy-done | bytes 2064408
  2.2 0.0 copy-start.1
  2.2 1.0 %copy-done.1 = bf16[1,1024,168]{1,2,0:T(8,128)(2,1)S(1)} copy-done((bf16[1,1024,168]{1,2,0:T(8,128)(2,1)S(1)}, bf16[1,1024,168]{1,2,0:T(8,128)(2,1)}, u32[]{:S(2)}) %copy-start.1) | copy-done | bytes 344088
  3.2 0.0 copy-start.2
  3.2 0.8 copy-done.2
  4.0 0.0 copy-start.3
  4.0 0.8 copy-done.3
  4.7 0.0 copy-start.4
  4.8 0.8 copy-done.4
  5.5 88.8 %broadcast_grads.1 = (bf16[1,168,1024]{2,1,0:T(8,128)(2,1)S(1)}, bf16[1,168,6144]{2,1,0:T(8,128)(2,1)S(1)}, f32[4,128]{1,0:T(4,128)S(1)}) custom-call(bf16[192,128]{1,0:T(8,128)(2,1)S(1)} %bitcast.9, bf16[1,168,1024]{2,1,0:T(8,128)(2,1)S(1)} %bitcast.8, bf16[1,168,6144]{2,1,0:T(8,128)(2,1)S(1)} %copy-done, s32[4,2048]{1,0:T(4,128)S(1)} %bitcast.10, ...), custom_call_target="tpu_custom_call" | custom-call | flops 8000000000 | bytes 30000000 | tf_op jit(solution)/shard_map/broadcast_grads/pallas_call | solution.py:334
  94.3 0.7 copy.11
  95.0 1.3 %copy.12 = bf16[1,168,6144]{2,1,0:T(8,128)(2,1)} copy(bf16[1,168,6144]{2,1,0:T(8,128)(2,1)S(1)} %get-tuple-element.13) | data formatting | bytes 4128768
  96.3 0.6 copy.13
Async XLA Ops:
  0.6 1.6 %copy-start = (bf16[1,168,6144]{2,1,0:T(8,128)(2,1)S(1)}, bf16[1,168,6144]{2,1,0:T(8,128)(2,1)}, u32[]{:S(2)}) copy-start(bf16[1,168,6144]{2,1,0:T(8,128)(2,1)} %w_hbm.1) | copy-start | bytes 6193156
  2.2 1.0 %copy-start.1 = (bf16[1,1024,168]{1,2,0:T(8,128)(2,1)S(1)}, bf16[1,1024,168]{1,2,0:T(8,128)(2,1)}, u32[]{:S(2)}) copy-start(bf16[1,1024,168]{1,2,0:T(8,128)(2,1)} %param.6) | copy-start | bytes 1032196
  3.2 0.8 copy-start.2
  4.0 0.8 copy-start.3
  4.7 0.8 copy-start.4

commit v3 on v2

--- a/solution.py
+++ b/solution.py
@@ -1,3 +1,5 @@
+import functools
+
 import jax
 import jax.numpy as jnp
 from jax import lax
@@ -19,17 +21,17 @@
 GROUPS = 9
 NT = (((1,), (1,)), ((), ()))
 ORDER = (0, 1, 3, 2)
-EARLY = (0, 1, 2)
-EARLY_SLOTS = (0, 1, 2, 3, 4)
-SKIP = 4
-LATE = (4, 7, 8)
+EARLY = (0, 1, 2, 3)
+EARLY_SLOTS = (0, 1, 2, 3, 4, 5, 6)
+SKIP = 5
+LATE = (5, 7, 8)
 
 PLAN = (
-    "U1", "U3", "Z10", "U2", "Z11", "Z13", "P0", "Z12", "Z20", "Z21", "Z23", "L0", "Z22", "P1", "Z30", "Z31", "R0",
-    "Z33", "G0", "Z32", "P2", "Z40", "L1", "Z41", "Z43", "Z42", "R1", "Z50", "Z51", "P3", "Z53", "G1", "Z52", "L2",
-    "E0", "Z60", "Z61", "L3", "R2", "Z63", "Z62", "R3", "P5", "Z70", "E1", "F0", "G2", "Z71", "E2", "G3", "Z73", "Z72",
-    "Z80", "P6", "E3", "F1", "L5", "Z81", "E4", "Z83", "F2", "Z82", "R5", "P7", "E5", "F3", "G5", "L6", "F4", "P8",
-    "R6", "F5", "L7", "G6", "L8", "R4", "R7", "R8",
+    "U1", "U3", "Z10", "U2", "Z11", "Z13", "P0", "Z12", "Z20", "Z21", "Z23", "L0", "Z22", "P1", "Z30", "Z31", "Z33",
+    "R0", "Z32", "P2", "Z40", "L1", "G0", "Z41", "Z43", "Z42", "R1", "Z50", "P3", "Z51", "Z53", "L2", "G1", "Z52",
+    "Z60", "R2", "Z61", "P4", "Z63", "G2", "Z62", "L3", "Z70", "E0", "Z71", "E1", "Z73", "L4", "R3", "Z72", "G3", "Z80",
+    "R4", "E2", "G4", "P6", "Z81", "F0", "E3", "Z83", "F1", "Z82", "E4", "P7", "F2", "E5", "L6", "F3", "P8", "R6", "F4",
+    "G6", "L7", "F5", "L8", "R7", "R5", "R8",
 )
 
 
@@ -65,6 +67,7 @@
             ((ex_hbm, ex_ref), (rw_hbm, rw_ref), (hid_hbm, hid_ref), (w_hbm, w_ref))
         )
     ]
+    loads.append(pltpu.make_async_copy(og_ref, rows.at[0, c, v, u], load.at[4]))
     for op in loads:
         op.start()
 
@@ -201,43 +204,52 @@
     def columns(zi):
         return pl.ds(pl.multiple_of(zi * FEAT, 128), FEAT)
 
+    def block(s, xx, yh, core):
+        if core == 0:
+            return rows[s, 0, xx, 2 * yh : 2 * yh + 2].reshape(FEAT, TOK)
+        return jnp.concatenate([rows[s, 1, 2 * yh, xx], rows[s, 1, 2 * yh + 1, xx]], axis=0)
+
     def slab(s, xx):
-        cols = []
-        for b in range(4):
-            yh = b // 2
-            if b % 2 == 0:
-                cols.append(rows[s, 0, xx, 2 * yh : 2 * yh + 2].reshape(FEAT, TOK))
-            else:
-                cols.append(jnp.concatenate([rows[s, 1, 2 * yh, xx], rows[s, 1, 2 * yh + 1, xx]], axis=0))
-        return jnp.concatenate(cols, axis=1)
+        return jnp.concatenate([block(s, xx, b // 2, b % 2) for b in range(4)], axis=1)
 
     def add_raw(d, first):
         here = places(d)
         w = jnp.concatenate([w_ref[0, :, columns(zi)] for _, zi in here], axis=1)
 
-        def tile(xx, _):
+        for xx in range(4):
             t = jnp.concatenate([slab(s, xx) for s, _ in here], axis=0)
-            tokens = pl.ds(pl.multiple_of(xx * 4 * TOK, 4 * TOK), 4 * TOK)
+            tokens = pl.ds(xx * 4 * TOK, 4 * TOK)
             more = jnp.dot(w, t, preferred_element_type=F32)
             raw[:, tokens] = more if first else raw[:, tokens] + more
-            return 0
-
-        lax.fori_loop(0, 4, tile, 0)
+
+    def add_last(core):
+        w = w_ref[0, :, columns((z + 8) % Z)]
+
+        for xx in range(4):
+            t = jnp.concatenate([block(15, xx, yh, core) for yh in (0, 1)], axis=1)
+            more = jnp.dot(w, t, preferred_element_type=F32)
+            for yh in (0, 1):
+                tokens = pl.ds((4 * xx + 2 * yh + core) * TOK, TOK)
+                raw[:, tokens] += more[:, yh * TOK : (yh + 1) * TOK]
 
     def put_grad(d):
-        for s, zi in places(d):
-            t = jnp.concatenate([slab(s, xx) for xx in range(4)], axis=1)
-            wg_ref[0, :, columns(zi)] = lax.dot_general(hw[...], t, NT, preferred_element_type=F32).astype(BF16)
+        here = places(d)
+        t = jnp.concatenate(
+            [jnp.concatenate([slab(s, xx) for xx in range(4)], axis=1) for s, _ in here], axis=0
+        )
+        grad = lax.dot_general(hw[...], t, NT, preferred_element_type=F32).astype(BF16)
+        for i, (_, zi) in enumerate(here):
+            wg_ref[0, :, columns(zi)] = grad[:, i * FEAT : (i + 1) * FEAT]
 
     for k in (1, 3, 2):
         push(og_ref, piece(0, v, 0), u_s.at[k - 1], u_r.at[k - 1], along(k, 0))
     z_send(0, 0)
     v_piece(0, 0)
-    rows[0, c, v, u] = og_ref[...]
     for op in loads[:3]:
         op.wait()
     prepare()
-    loads[3].wait()
+    for op in loads[3:]:
+        op.wait()
 
     def on_u(k):
         arrived(piece(0, v, k), u_s.at[k - 1], u_r.at[k - 1])
@@ -287,6 +299,8 @@
             e_send(d)
         elif kind == "F":
             on_e(d)
+        elif kind == "R" and d == 8:
+            continue
         elif kind == "R":
             c_wait(d)
             add_raw(d, not summed)
@@ -294,12 +308,23 @@
         else:
             put_grad(d)
 
-    share = jnp.sum(ht[...].astype(F32) * raw[...], axis=0, keepdims=True)
-    for b in range(BLOCKS):
-        sg[b] = jnp.broadcast_to(share[:, b * TOK : (b + 1) * TOK], (8, TOK))
-    for k in range(1, BLOCKS):
-        to = (ex + k) % BLOCKS
-        push(sg.at[to], sgx.at[ex], x_s.at[k], x_r.at[k], {"dp": dp, "expert": to})
+    def tell(core, first):
+        for i in range(BLOCKS // 2):
+            b = 2 * i + core
+            tokens = pl.ds(pl.multiple_of(b * TOK, TOK), TOK)
+            share = jnp.sum(ht[:, tokens].astype(F32) * raw[:, tokens], axis=0, keepdims=True)
+            sg[b] = jnp.broadcast_to(share, (8, TOK))
+        for k in range(first, BLOCKS, 2):
+            to = (ex + k) % BLOCKS
+            push(sg.at[to], sgx.at[ex], x_s.at[k], x_r.at[k], {"dp": dp, "expert": to})
+
+    for core in (0, 1):
+        pl.when(c == core)(functools.partial(add_last, core))
+    tell(c, 2)
+    c_wait(8)
+    for core in (0, 1):
+        pl.when(c != core)(functools.partial(add_last, core))
+    tell(1 - c, 1)
     sgx[ex] = sg[ex]
     for d in LATE[::2]:
         put_grad(d)
@@ -310,7 +335,8 @@
     for e in range(BLOCKS):
         total = total + jnp.where(named == e, sgx[e, 0:1, :], 0.0)
     red[dp] = total
-    for k in range(1, 2 * Z):
+    before = len(sent)
+    for k in sorted(range(1, 2 * Z), key=lambda k: -min(k, 2 * Z - k)):
         push(red.at[dp], red.at[dp], d_s.at[k], d_r.at[k], {"dp": (dp + k) % (2 * Z), "expert": ex})
     for d in LATE[1::2]:
         put_grad(d)
@@ -318,19 +344,22 @@
         tokens = pl.ds(j * 2 * TOK, 2 * TOK)
         grad = (raw[:, tokens] * wtok[:, tokens]).astype(BF16)
         hg_ref[0, :, pl.ds(j * TOK, TOK)] = lax.dot_general(grad, sel[j], NT, preferred_element_type=F32).astype(BF16)
+    for op in sent[:before]:
+        op.wait_send()
     for k in range(1, 2 * Z):
         arrived(red.at[(dp - k + 2 * Z) % (2 * Z)], d_s.at[k], d_r.at[k])
     total = red[0]
     for k in range(1, 2 * Z):
         total = total + red[k]
     rt_ref[...] = total
-    for op in sent:
+    for op in sent[before:]:
         op.wait_send()
 
 
 def body(out_grad, hidden, down_weight, experts, route_weight):
     vmem = pl.BlockSpec(memory_space=pltpu.VMEM)
     dma = pltpu.SemaphoreType.DMA
+    operands = (out_grad.T, hidden.swapaxes(1, 2), down_weight, experts.T, route_weight.T)
     hidden_grad, weight_grad, route = pl.pallas_call(
         kernel,
         out_shape=(
@@ -338,7 +367,7 @@
             jax.ShapeDtypeStruct(down_weight.shape, BF16),
             jax.ShapeDtypeStruct((4, TOK), F32),
         ),
-        in_specs=[vmem] + [pl.BlockSpec(memory_space=pltpu.HBM)] * 4,
+        in_specs=[pl.BlockSpec(memory_space=pltpu.HBM)] * 5,
         out_specs=(vmem,) * 3,
         scratch_shapes=[
             pltpu.VMEM((1, FFD, BLOCKS * MOST), BF16),
@@ -354,10 +383,10 @@
             pltpu.VMEM((BLOCKS, 8, TOK), F32),
             pltpu.VMEM((BLOCKS, 8, TOK), F32),
             pltpu.VMEM((2 * Z, 4, TOK), F32),
-            dma((4,)),
+            dma((5,)),
             dma((3,)), dma((3,)),
             dma((8, 2, 4)), dma((8, 2, 4)),
-            dma((5, 4, 2)), dma((5, 4, 2)),
+            dma((7, 4, 2)), dma((7, 4, 2)),
             dma((2, 6)), dma((2, 6)),
             dma((GROUPS, 2)), dma((GROUPS, 2)),
             dma((GROUPS, 2)), dma((GROUPS, 2)),
@@ -370,7 +399,7 @@
         ),
         cost_estimate=pl.CostEstimate(flops=8 * 10**9, bytes_accessed=30 * 10**6, transcendentals=0),
         name="broadcast_grads",
-    )(out_grad.T, hidden.swapaxes(1, 2), down_weight, experts.T, route_weight.T)
+    )(*(pltpu.with_memory_space_constraint(a, pltpu.HBM) for a in operands))
     return hidden_grad.swapaxes(1, 2), weight_grad, route.T
 
 

time: 97.5 us -> 89.5 us (0.918)
  local copies, waits for them, and re-layouts: 7.48 us -> 2.61 us
  Pallas kernels: 88.8 us -> 86.1 us
    unnamed x13 -> x3, local copies, waits for them, and re-layouts: 7.48 us -> 2.61 us
    pallas_call x1, Pallas kernels: 88.8 us -> 86.1 us  [body(): pl.pallas_call(kernel, out_shape=(jax.ShapeDtypeStruct((1, FFD, BLOCKS *...]
where the time goes in v3:
time: 89.5 us; the launch traced here: 89.4 us
  Pallas kernels  86.1 us (96%)
  local copies, waits for them, and re-layouts  2.61 us (3%)
    pallas_call x1, Pallas kernels, body(): pl.pallas_call(kernel, out_shape=(jax.ShapeDtypeStruct((1, FFD, BLOCKS *...  86.1 us
    unnamed x3, local copies, waits for them, and re-layouts  2.61 us

profile of v3, /device:TPU:1, one launch (start us, length us, event | category | flops | bytes accessed | tf_op | source)
XLA Modules:
  0.0 89.4 jit_solution(10908001617181369038)
XLA Ops:
  0.6 86.1 %broadcast_grads.1 = (bf16[1,168,1024]{2,1,0:T(8,128)(2,1)S(1)}, bf16[1,168,6144]{2,1,0:T(8,128)(2,1)S(1)}, f32[4,128]{1,0:T(4,128)S(1)}) custom-call(bf16[192,128]{1,0:T(8,128)(2,1)} %bitcast.9, bf16[1,168,1024]{2,1,0:T(8,128)(2,1)} %bitcast.8, bf16[1,168,6144]{2,1,0:T(8,128)(2,1)} %w_hbm.1, s32[4,2048]{1,0:T(4,128)} %bitcast.10, f32[4,2048]{1,0:T(4,128)} %bitcast.11), custom_call_target="tpu_custom_call" | custom-call | flops 8000000000 | bytes 30000000 | tf_op jit(solution)/shard_map/broadcast_grads/pallas_call | solution.py:363
  86.8 0.7 copy.11
  87.5 1.3 %copy.12 = bf16[1,168,6144]{2,1,0:T(8,128)(2,1)} copy(bf16[1,168,6144]{2,1,0:T(8,128)(2,1)S(1)} %get-tuple-element.13) | data formatting | bytes 4128768
  88.8 0.6 copy.13

commit v4 on v3

--- a/solution.py
+++ b/solution.py
@@ -61,6 +61,11 @@
 
     twin = at(x, y, z, 1 - c)
 
+    barrier = pltpu.get_barrier_semaphore()
+    greeted = [along(k, 0) for k in (1, 2, 3)] + [along(0, k) for k in (1, 3)]
+    greeted += [beside(1), beside(-1), twin]
+    for device in greeted:
+        pl.semaphore_signal(barrier, inc=1, device_id=device, device_id_type=MESH)
     loads = [
         pltpu.make_async_copy(src, dst, load.at[i])
         for i, (src, dst) in enumerate(
@@ -70,13 +75,8 @@
     loads.append(pltpu.make_async_copy(og_ref, rows.at[0, c, v, u], load.at[4]))
     for op in loads:
         op.start()
-
-    barrier = pltpu.get_barrier_semaphore()
-    greeted = [along(k, 0) for k in (1, 2, 3)] + [along(0, k) for k in (1, 3)]
-    greeted += [beside(1), beside(-1), twin]
-    for device in greeted:
-        pl.semaphore_signal(barrier, inc=1, device_id=device, device_id_type=MESH)
     pl.semaphore_wait(barrier, len(greeted))
+    loads[4].wait()
 
     sent = []
 
@@ -103,8 +103,7 @@
                 continue
             src = 0 if d == 0 else 2 * d - 1 + way
             dst = 15 if d == 7 else 2 * d + 1 + way
-            own = og_ref if d == 0 and k == 0 else piece(src, v, k)
-            push(own, piece(dst, v, k), z_s.at[d, way, k], z_r.at[d, way, k], beside(1 - 2 * way))
+            push(piece(src, v, k), piece(dst, v, k), z_s.at[d, way, k], z_r.at[d, way, k], beside(1 - 2 * way))
 
     def z_wait(d, k):
         for way in (0, 1):
@@ -135,8 +134,7 @@
     def v_piece(slot, k):
         at_slot = EARLY_SLOTS.index(slot)
         for way in (0, 1):
-            own = og_ref if slot == 0 and k == 0 else piece(slot, v, k)
-            push(own, piece(slot, v, k), p_s.at[at_slot, k, way], p_r.at[at_slot, k, way], along(0, 1 - 2 * way))
+            push(piece(slot, v, k), piece(slot, v, k), p_s.at[at_slot, k, way], p_r.at[at_slot, k, way], along(0, 1 - 2 * way))
 
     def v_pass(d):
         for way in (0, 1):
@@ -242,14 +240,13 @@
             wg_ref[0, :, columns(zi)] = grad[:, i * FEAT : (i + 1) * FEAT]
 
     for k in (1, 3, 2):
-        push(og_ref, piece(0, v, 0), u_s.at[k - 1], u_r.at[k - 1], along(k, 0))
+        push(piece(0, v, 0), piece(0, v, 0), u_s.at[k - 1], u_r.at[k - 1], along(k, 0))
     z_send(0, 0)
     v_piece(0, 0)
     for op in loads[:3]:
         op.wait()
     prepare()
-    for op in loads[3:]:
-        op.wait()
+    loads[3].wait()
 
     def on_u(k):
         arrived(piece(0, v, k), u_s.at[k - 1], u_r.at[k - 1])
@@ -356,17 +353,29 @@
         op.wait_send()
 
 
+def hand_over(hg_ref, wg_ref, rt_ref, hg_out, wg_out, rt_out, sems):
+    width = wg_ref.shape[2] // 4
+    copies = [(wg_ref.at[:, :, pl.ds(i * width, width)], wg_out.at[:, :, pl.ds(i * width, width)]) for i in range(4)]
+    copies += [(hg_ref, hg_out), (rt_ref, rt_out)]
+    copies = [pltpu.make_async_copy(src, dst, sems.at[i]) for i, (src, dst) in enumerate(copies)]
+    for op in copies:
+        op.start()
+    for op in copies:
+        op.wait()
+
+
 def body(out_grad, hidden, down_weight, experts, route_weight):
     vmem = pl.BlockSpec(memory_space=pltpu.VMEM)
     dma = pltpu.SemaphoreType.DMA
     operands = (out_grad.T, hidden.swapaxes(1, 2), down_weight, experts.T, route_weight.T)
-    hidden_grad, weight_grad, route = pl.pallas_call(
+    shapes = (
+        jax.ShapeDtypeStruct((1, FFD, BLOCKS * MOST), BF16),
+        jax.ShapeDtypeStruct(down_weight.shape, BF16),
+        jax.ShapeDtypeStruct((4, TOK), F32),
+    )
+    results = pl.pallas_call(
         kernel,
-        out_shape=(
-            jax.ShapeDtypeStruct((1, FFD, BLOCKS * MOST), BF16),
-            jax.ShapeDtypeStruct(down_weight.shape, BF16),
-            jax.ShapeDtypeStruct((4, TOK), F32),
-        ),
+        out_shape=shapes,
         in_specs=[pl.BlockSpec(memory_space=pltpu.HBM)] * 5,
         out_specs=(vmem,) * 3,
         scratch_shapes=[
@@ -400,6 +409,15 @@
         cost_estimate=pl.CostEstimate(flops=8 * 10**9, bytes_accessed=30 * 10**6, transcendentals=0),
         name="broadcast_grads",
     )(*(pltpu.with_memory_space_constraint(a, pltpu.HBM) for a in operands))
+    hidden_grad, weight_grad, route = pl.pallas_call(
+        hand_over,
+        out_shape=shapes,
+        in_specs=[pl.BlockSpec(memory_space=pl.ANY)] * 3,
+        out_specs=(pl.BlockSpec(memory_space=pltpu.HBM),) * 3,
+        scratch_shapes=[dma((6,))],
+        compiler_params=pltpu.CompilerParams(vmem_limit_bytes=1 << 20),
+        name="hand_over",
+    )(*results)
     return hidden_grad.swapaxes(1, 2), weight_grad, route.T
 
 

time: 89.5 us -> 88.2 us (0.985)
  local copies, waits for them, and re-layouts: 2.61 us -> 0 us
  Pallas kernels: 86.1 us -> 87.3 us
    unnamed x3 -> x0, local copies, waits for them, and re-layouts: 2.61 us -> none
    pallas_call x1 -> x2, Pallas kernels: 86.1 us -> 87.3 us  [the longest x1 85.8 us: body(): pl.pallas_call(kernel, out_shape=shapes, in_specs=[pl.BlockSpec(memory_sp...]
where the time goes in v4:
time: 88.2 us; the launch traced here: 88.1 us
  Pallas kernels  87.3 us (99%)
    pallas_call x1, Pallas kernels, body(): pl.pallas_call(kernel, out_shape=shapes, in_specs=[pl.BlockSpec(memory_sp...  85.8 us

profile of v4, /device:TPU:1, one launch (start us, length us, event | category | flops | bytes accessed | tf_op | source)
XLA Modules:
  0.0 88.1 jit_solution(13990383123963094928)
XLA Ops:
  0.6 85.8 %broadcast_grads.1 = (bf16[1,168,1024]{2,1,0:T(8,128)(2,1)S(1)}, bf16[1,168,6144]{2,1,0:T(8,128)(2,1)S(1)}, f32[4,128]{1,0:T(4,128)S(1)}) custom-call(bf16[192,128]{1,0:T(8,128)(2,1)} %bitcast.8, bf16[1,168,1024]{2,1,0:T(8,128)(2,1)} %bitcast.6, bf16[1,168,6144]{2,1,0:T(8,128)(2,1)} %w_hbm.1, s32[4,2048]{1,0:T(4,128)} %bitcast.9, f32[4,2048]{1,0:T(4,128)} %bitcast.10), custom_call_target="tpu_custom_call" | custom-call | flops 8000000000 | bytes 30000000 | tf_op jit(solution)/shard_map/broadcast_grads/pallas_call | solution.py:376
  86.4 1.5 %hand_over.1 = (bf16[1,168,1024]{2,1,0:T(8,128)(2,1)}, bf16[1,168,6144]{2,1,0:T(8,128)(2,1)}, f32[4,128]{1,0:T(4,128)}) custom-call(bf16[1,168,1024]{2,1,0:T(8,128)(2,1)S(1)} %get-tuple-element.9.hg_ref, bf16[1,168,6144]{2,1,0:T(8,128)(2,1)S(1)} %get-tuple-element.10.wg_ref, f32[4,128]{1,0:T(4,128)S(1)} %get-tuple-element.11.rt_ref), custom_call_target="tpu_custom_call" | custom-call | tf_op jit(solution)/shard_map/hand_over/pallas_call | solution.py:412

commit v5 on v4

--- a/solution.py
+++ b/solution.py
@@ -40,7 +40,7 @@
     hg_ref, wg_ref, rt_ref,
     hid_ref, w_ref, ex_ref, rw_ref,
     rows, raw, ht, hw, sel, wtok, sg, sgx, red,
-    load, u_s, u_r, z_s, z_r, p_s, p_r, e_s, e_r, v_s, v_r, a_s, a_r, c_s, c_r, x_s, x_r, d_s, d_r,
+    load, u_s, u_r, z_s, z_r, p_s, p_r, e_s, e_r, v_s, v_r, a_s, a_r, f_s, f_r, c_s, c_r, x_s, x_r, d_s, d_r,
 ):
     dp, ex = lax.axis_index("dp"), lax.axis_index("expert")
     z, ylo = dp // 2, dp % 2
@@ -52,9 +52,9 @@
     def at(x, y, z, c):
         return {"dp": z * 2 + y % 2, "expert": (x * 2 + y // 2) * 2 + c}
 
-    def along(du, dv):
+    def along(du, dv, core=c):
         uu, vv = (u + du + 4) % 4, (v + dv + 4) % 4
-        return at(vv + c * (uu - vv), uu + c * (vv - uu), z, c)
+        return at(vv + c * (uu - vv), uu + c * (vv - uu), z, core)
 
     def beside(dz):
         return at(x, y, (z + dz + Z) % Z, c)
@@ -149,6 +149,11 @@
                 arrived(v_all(d, vv), v_s.at[d, way], v_r.at[d, way])
             half = v_half(d, vv, way)
             push(half, half, a_s.at[d, way], a_r.at[d, way], along(0, step))
+        if d == 8:
+            for way in (0, 1):
+                step = 1 - 2 * way
+                half = v_half(d, (v - step + 4) % 4, way)
+                push(half, half, f_s.at[way], f_r.at[way], along(0, step, 1 - c))
 
     def v_last(d):
         for way in (0, 1):
@@ -171,7 +176,7 @@
         push(own, own, c_s.at[d, k], c_r.at[d, k], twin)
 
     def c_wait(d):
-        for k in range(4):
+        for k in (0, 1, 3) if d == 8 else (0, 1, 2, 3):
             arrived(rows.at[slots(d), 1 - c, (u + k) % 4], c_s.at[d, k], c_r.at[d, k])
 
     def prepare():
@@ -274,7 +279,8 @@
 
     def on_far(d):
         v_last(d)
-        c_send(d, 2)
+        if d < 8:
+            c_send(d, 2)
 
     def on_e(unit):
         e_wait(unit)
@@ -319,6 +325,8 @@
         pl.when(c == core)(functools.partial(add_last, core))
     tell(c, 2)
     c_wait(8)
+    for way in (0, 1):
+        arrived(rows.at[slots(8), 1 - c, (u + 2) % 4, pl.ds(2 * way, 2)], f_s.at[way], f_r.at[way])
     for core in (0, 1):
         pl.when(c != core)(functools.partial(add_last, core))
     tell(1 - c, 1)
@@ -399,6 +407,7 @@
             dma((2, 6)), dma((2, 6)),
             dma((GROUPS, 2)), dma((GROUPS, 2)),
             dma((GROUPS, 2)), dma((GROUPS, 2)),
+            dma((2,)), dma((2,)),
             dma((GROUPS, 4)), dma((GROUPS, 4)),
             dma((BLOCKS,)), dma((BLOCKS,)),
             dma((2 * Z,)), dma((2 * Z,)),

time: 88.2 us -> 88.2 us (level)
  no operation moved by 1% of the time
where the time goes in v5:
time: 88.2 us; the launch traced here: 88.1 us
  Pallas kernels  87.3 us (99%)
    pallas_call x1, Pallas kernels, body(): pl.pallas_call(kernel, out_shape=shapes, in_specs=[pl.BlockSpec(memory_sp...  85.8 us

profile of v5, /device:TPU:1, one launch (start us, length us, event | category | flops | bytes accessed | tf_op | source)
XLA Modules:
  0.0 88.1 jit_solution(1488200275733320942)
XLA Ops:
  0.6 85.8 %broadcast_grads.1 = (bf16[1,168,1024]{2,1,0:T(8,128)(2,1)S(1)}, bf16[1,168,6144]{2,1,0:T(8,128)(2,1)S(1)}, f32[4,128]{1,0:T(4,128)S(1)}) custom-call(bf16[192,128]{1,0:T(8,128)(2,1)} %bitcast.8, bf16[1,168,1024]{2,1,0:T(8,128)(2,1)} %bitcast.6, bf16[1,168,6144]{2,1,0:T(8,128)(2,1)} %w_hbm.1, s32[4,2048]{1,0:T(4,128)} %bitcast.9, f32[4,2048]{1,0:T(4,128)} %bitcast.10), custom_call_target="tpu_custom_call" | custom-call | flops 8000000000 | bytes 30000000 | tf_op jit(solution)/shard_map/broadcast_grads/pallas_call | solution.py:384
  86.5 1.5 %hand_over.1 = (bf16[1,168,1024]{2,1,0:T(8,128)(2,1)}, bf16[1,168,6144]{2,1,0:T(8,128)(2,1)}, f32[4,128]{1,0:T(4,128)}) custom-call(bf16[1,168,1024]{2,1,0:T(8,128)(2,1)S(1)} %get-tuple-element.9.hg_ref, bf16[1,168,6144]{2,1,0:T(8,128)(2,1)S(1)} %get-tuple-element.10.wg_ref, f32[4,128]{1,0:T(4,128)S(1)} %get-tuple-element.11.rt_ref), custom_call_target="tpu_custom_call" | custom-call | tf_op jit(solution)/shard_map/hand_over/pallas_call | solution.py:421
